TPU v7x, 128 devices: a whole 4x4x4 slice. The times are simulated.
128 devices in a mesh: gx: 8 (over x, core), gy: 16 (over y, z).
Axes of the slice: x: 4, y: 4, z: 4, core: 2. Of those that a mesh axis runs over, the one named last changes fastest.
Arguments:
- gcm_state: float32 [64, 256, 144], P('gx', 'gy'), may hold values from -6 to 6
- crm_state: bfloat16 [128, 128, 2, 2, 3712], P(('gx', 'gy')), may hold values from -6 to 6
- owners: int32 [128, 128, 1], P(('gx', 'gy')), may hold values from 0 to 127; in each aligned block of 128 rows (0 to 127, 128 to 255, ..., all dimensions but the last counted through in order) at most 2 rows name the same one
- ice_mask: int32 [64, 256, 58], P('gx', 'gy'), may hold values 0 or 1
- horizontal_operator: bfloat16 [2, 64, 64], replicated, may hold values from -1 to 2
- vertical_inverse: bfloat16 [2, 58, 58], replicated, may hold values from -1 to 2
- diffusivity: float32 [144], replicated, may hold values from 0.02 to 0.2
Outputs:
- gcm_out: float32 [64, 256, 144], P('gx', 'gy')
- crm_out: bfloat16 [128, 128, 2, 2, 3712], P(('gx', 'gy'))
Inputs may be any that keep to these rules, and one draw needn't show every extreme that they name: `owners`: among one device's columns at most 2 name the same owner, a bound that some block reaches.
All inputs are finite; a program needn't handle non-finite values. No bound on the sum of `ice_mask` on one device may be relied on, other than what follows from the above.
Results may differ from a plain program's by a relative error of at most 0.0055.
Values may be sent and summed in bfloat16 or wider, within the bound.
A program may use at most 64 MiB of HBM per device.

v0:
```python
import jax
import jax.numpy as jnp
from jax import lax
from jax.experimental import pallas as pl
from jax.experimental.pallas import tpu as pltpu
from jax.sharding import PartitionSpec as P

BF, F32 = jnp.bfloat16, jnp.float32
SUBSTEPS, CLEV, CX, LEV, COLS = 4, 58, 64, 72, 128
BLOCKS, GROUP, ROWS = 32, 4, 464
NX, NY, WIDTH = 8, 16, 144
VMEM_MIB = 58
MESH = pl.DeviceIdType.MESH


def iota(shape, dim):
    return lax.broadcasted_iota(jnp.int32, shape, dim)


def level_of(lane):
    place = lane % 64
    return place % 32 * 2 + place // 32


def hat(rows, cols, ratio):
    gap = rows.astype(F32) * ratio - cols.astype(F32)
    return jnp.maximum(0.0, 1.0 - jnp.abs(gap))


def dot(a, b, ca=1, cb=0):
    return lax.dot_general(a, b, (((ca,), (cb,)), ((), ())), preferred_element_type=F32)


def onehots(owners_row, row_owner):
    o, c = iota((COLS, COLS), 0), iota((COLS, COLS), 1)
    same = jnp.where(owners_row == row_owner(o), 1.0, 0.0)
    rank = dot(same.astype(BF), jnp.where(o < c, 1.0, 0.0).astype(BF))
    first = jnp.where(rank < 0.5, same, 0.0)
    return first.astype(BF), (same - first).astype(BF)


def outgoing(gcm, ice, m0, m1):
    low = gcm.astype(BF)
    ice = ice.astype(F32).astype(BF)
    row, lane = iota((WIDTH, 384), 0), iota((WIDTH, 384), 1)
    level = level_of(lane)
    weight = jnp.where(
        (lane // 128 == row // LEV) & (level < CLEV), hat(level, row % LEV, (LEV - 1) / (CLEV - 1)), 0.0
    )
    row2, lane2 = iota((CLEV, 384), 0), iota((CLEV, 384), 1)
    pick = jnp.where((lane2 >= 256) & (level_of(lane2) == row2), 1.0, 0.0)
    lane1 = iota((1, 384), 1)
    drive = dot(low, weight.astype(BF)) + dot(ice, pick.astype(BF)) + jnp.where(lane1 >= 256, 2.0, 0.0)
    drive = drive.astype(BF)
    return jnp.where(iota((COLS, 384), 1) // 64 % 2 == 0, dot(m0, drive), dot(m1, drive)).astype(BF)


def operators(h_ref, v_ref, hb_ref, vb_ref):
    a, b = iota((256, 256), 0) // 64, iota((256, 256), 1) // 64
    diag = a == b
    tile = jnp.where(iota((256, CX), 0) % 64 == iota((256, CX), 1), 1.0, 0.0).astype(BF)
    rows = jnp.where(level_of(iota((256, CLEV), 0)) == iota((256, CLEV), 1), 1.0, 0.0).astype(BF)
    for v in range(2):
        h = (h_ref[v].astype(F32) - 1.0 / 256.0).astype(BF)
        hb_ref[v] = jnp.where(diag, dot(dot(tile, h).astype(BF), tile, 1, 1), 0.0).astype(BF)
    v0 = dot(dot(rows, v_ref[0]).astype(BF), rows, 1, 1)
    v1 = dot(dot(rows, v_ref[1]).astype(BF), rows, 1, 1)
    vb_ref[...] = jnp.where(diag, jnp.where(a < 2, v0, v1), 0.0).astype(BF)


def place():
    return lax.axis_index("gx"), lax.axis_index("gy")


def device(index):
    return (index // NY, index % NY)


def rolled(a, b, low):
    return jnp.where(low, a, pltpu.roll(b, 64, 1)), jnp.where(low, pltpu.roll(a, 64, 1), b)


def slot_rows(j, h, i, v, count):
    return pl.ds(58 * ((2 * h + i) * 2 + j) + v, count, stride=2)


def unpack(g, x_s, old_s, sx):
    low = iota((32, 128), 1) < 64
    for k in range(GROUP):
        sx[k, pl.ds(0, ROWS), :] = x_s[g, pl.ds(k * ROWS, ROWS), :].astype(F32)
    for k in range(GROUP):
        for v in range(2):
            piece = {}
            for j in range(2):
                for h in range(2):
                    d = [sx[k, slot_rows(j, h, i, v, 32), :] for i in range(2)]
                    piece[j, 0, h], piece[j, 1, h] = rolled(d[0], d[1], low)
            x0 = jnp.concatenate(
                [jnp.concatenate([piece[j, p, 0], piece[j, p, 1]], axis=1) for j in range(2) for p in range(2)], axis=0
            )
            old_s[g, k, v] = x0.astype(BF)


def evolve(g, arr_s, old_s, hb_s, vb_s, x_s, tend_s, sx):
    low = iota((32, 128), 1) < 64
    ind = jnp.where(iota((8, 256), 0) == iota((8, 256), 1) // 64, 1.0, 0.0).astype(BF)
    spread = ind[0:4, :]
    forces, flags = [[], []], []
    for k in range(GROUP):
        arr = arr_s[pl.ds(g * NY + 4 * k, 4), 0, :].astype(BF)
        for v in range(2):
            forces[v].append(dot(arr[:, 128 * v : 128 * v + 128], spread, 0, 0) * 0.25)
        flags.append(dot(arr[:, 256:384], spread, 0, 0))
    state = [[old_s[g, k, v] for k in range(GROUP)] for v in range(2)]
    for step in range(SUBSTEPS):
        f = [dot(jnp.concatenate(state[v], axis=0), hb_s[v]) for v in range(2)]
        state = [[], []]
        for k in range(GROUP):
            f0 = f[0][k * 128 : (k + 1) * 128] + forces[0][k]
            f1 = f[1][k * 128 : (k + 1) * 128] + forces[1][k]
            e = f1 - 0.5 * f0
            soft = jnp.maximum(e, 0.0) + jnp.log(1.0 + jnp.exp(-jnp.abs(e)))
            q = jnp.where(flags[k] > 2.5, 0.2 * e, 0.4 * soft)
            y = jnp.concatenate([(f0 + 0.5 * q).astype(BF), (f1 - q).astype(BF)], axis=0)
            z = dot(vb_s[...], y).astype(BF)
            for v in range(2):
                state[v].append(z[v * 128 : (v + 1) * 128])
    for k in range(GROUP):
        old = [old_s[g, k, v] for v in range(2)]
        diff = jnp.concatenate([(state[v][k].astype(F32) - old[v].astype(F32)).astype(BF) for v in range(2)], axis=0)
        tend = dot(ind, diff, 1, 1) * (1.0 / 64.0)
        tend_s[pl.ds(g * NY + 4 * k, 4), 0, :] = tend[0:4].astype(BF).astype(F32)
        for v in range(2):
            final = jnp.where(flags[k] > 1.0, state[v][k].astype(F32), old[v].astype(F32))
            for j in range(2):
                for h in range(2):
                    a, b = [
                        final[(j * 2 + p) * 32 : (j * 2 + p + 1) * 32, h * 128 : (h + 1) * 128] for p in range(2)
                    ]
                    d = rolled(a, b, low)
                    for i in range(2):
                        sx[k, slot_rows(j, h, i, v, 29), :] = d[i][0:29]
        x_s[g, pl.ds(k * ROWS, ROWS), :] = sx[k, pl.ds(0, ROWS), :].astype(BF)


def push(src, dst, send, recv, to):
    return pltpu.make_async_remote_copy(
        src_ref=src, dst_ref=dst, send_sem=send, recv_sem=recv, device_id=to, device_id_type=MESH
    )


def settle(ref, sem):
    pltpu.make_async_copy(ref, ref, sem).wait()


def step_kernel(
    gcm_ref, own_ref, ice_ref, h_ref, v_ref, diff_ref, x_hbm, out_ref, crm_hbm,
    x_s, old_s, sx, hb_s, vb_s, send_s, arr_s, tend_s, ret_s, u_s, l_s, r_s, hx_s, hy_s, edge_s,
    load_m, store_m, send_m, arr_m, back_m, ret_m, hs_m, hr_m,
):
    a, b = place()
    me = a * NY + b
    loads = [
        pltpu.make_async_copy(x_hbm.at[pl.ds(g * GROUP * ROWS, GROUP * ROWS)], x_s.at[g], load_m.at[g])
        for g in range(NX)
    ]
    for c in loads:
        c.start()
    barrier = pltpu.get_barrier_semaphore()

    def greet(k, carry):
        pl.semaphore_signal(barrier, inc=1, device_id=device((me + k) % COLS), device_id_type=MESH)
        return carry

    lax.fori_loop(1, COLS, greet, 0, unroll=True)
    m0, m1 = onehots(own_ref[...], lambda o: o)
    send_s[:, 0, :] = outgoing(gcm_ref[...], ice_ref[...], m0, m1).astype(F32)
    sx[:, pl.ds(ROWS, 8), :] = jnp.zeros((GROUP, 8, 128), F32)
    arr_s[pl.ds(me, 1)] = send_s[pl.ds(me, 1)]
    operators(h_ref, v_ref, hb_s, vb_s)
    pl.semaphore_wait(barrier, COLS - 1)

    def spread(g, carry):
        row = (a + 2 * NX - 1 - g) % NX
        for k in range(NY):
            col = (b + k) % NY
            copy = push(send_s.at[row * NY + col], arr_s.at[me], send_m, arr_m.at[a], (row, col))
            if k:
                copy.start()
            else:
                pl.when(g < NX - 1)(copy.start)
        slab = (a + 1 + g) % NX
        settle(x_s.at[slab], load_m.at[slab])
        unpack(slab, x_s, old_s, sx)
        return carry

    lax.fori_loop(0, NX, spread, 0)

    def group(g, carry):
        slab = (a + 1 + g) % NX

        @pl.when(g < NX - 1)
        def _():
            settle(arr_s.at[pl.ds(0, NY)], arr_m.at[slab])

        @pl.when(g == NX - 1)
        def _():
            settle(arr_s.at[pl.ds(0, NY - 1)], arr_m.at[slab])

        evolve(slab, arr_s, old_s, hb_s, vb_s, x_s, tend_s, sx)
        pltpu.make_async_copy(
            x_s.at[slab], crm_hbm.at[pl.ds(pl.multiple_of(slab * GROUP * ROWS, 16), GROUP * ROWS)], store_m.at[slab]
        ).start()
        for k in range(NY):
            col = (b + k) % NY
            copy = push(tend_s.at[slab * NY + col], ret_s.at[me], back_m, ret_m, (slab, col))
            if k:
                copy.start()
            else:
                pl.when(g < NX - 1)(copy.start)
        return carry

    lax.fori_loop(0, NX, group, 0)
    ret_s[pl.ds(me, 1)] = tend_s[pl.ds(me, 1)]
    settle(send_s.at[pl.ds(0, COLS - 1)], send_m)
    row, col = iota((256, 256), 0), iota((256, 256), 1)
    level = level_of(row)
    grid = jnp.where(col >= LEV, col - LEV, col)
    lift = jnp.where(
        (row // 128 == jnp.where(col >= LEV, 1, 0)) & (level < CLEV) & (col < WIDTH),
        hat(grid, level, (CLEV - 1) / (LEV - 1)),
        0.0,
    ).astype(BF)
    lane = iota((COLS, 256), 1) // 64 % 2
    m0, m1 = onehots(own_ref[...], lambda o: o)
    settle(ret_s.at[pl.ds(0, COLS - 1)], ret_m)
    got = ret_s[:, 0, :].astype(BF)
    got = jnp.where(lane == 0, dot(m0, got, 0, 0), dot(m1, got, 0, 0)).astype(BF)
    gain = dot(got, lift)
    u_s[...] = gain.reshape(NX, NY, 256)
    u_s[:, :, 0:WIDTH] = (gain[:, 0:WIDTH] + gcm_ref[...]).reshape(NX, NY, WIDTH)
    for s in range(2):
        edge_s[s] = u_s[:, 15 * s, :]
    ends = [
        (u_s.at[NX - 1], hx_s.at[0], ((a + 1) % NX, b)),
        (u_s.at[0], hx_s.at[1], ((a + NX - 1) % NX, b)),
        (edge_s.at[1], hy_s.at[0], (a, (b + 1) % NY)),
        (edge_s.at[0], hy_s.at[1], (a, (b + NY - 1) % NY)),
    ]
    copies = [push(src, dst, hs_m.at[i], hr_m.at[i], to) for i, (src, dst, to) in enumerate(ends)]
    for c in copies:
        c.start()
    u = u_s[...].reshape(COLS, 256)
    l_s[...] = pltpu.roll(u, 1, 0).reshape(NX, NY, 256)
    r_s[...] = pltpu.roll(u, COLS - 1, 0).reshape(NX, NY, 256)
    settle(tend_s.at[pl.ds(0, COLS - 1)], back_m)
    for g in range(NX):
        settle(x_s.at[g], store_m.at[g])
    for c in copies:
        c.wait()
    l_s[:, 0, :] = hy_s[0]
    r_s[:, NY - 1, :] = hy_s[1]
    up = jnp.concatenate([hx_s[0], u[0:112]], axis=0)
    down = jnp.concatenate([u[16:128], hx_s[1]], axis=0)
    total = up + down + (l_s[...] + r_s[...]).reshape(COLS, 256) - 4.0 * u
    out_ref[...] = u[:, 0:WIDTH] + diff_ref[...] * total[:, 0:WIDTH]


def local(gcm_state, crm_state, owners, ice_mask, horizontal_operator, vertical_inverse, diffusivity):
    sds, vmem, dma = jax.ShapeDtypeStruct, pltpu.VMEM, pltpu.SemaphoreType.DMA
    x = crm_state.reshape(256, 2, 3712).transpose(0, 2, 1).reshape(7424, 128, 2).transpose(0, 2, 1).reshape(14848, 128)
    whole = pl.BlockSpec(memory_space=pltpu.VMEM)
    hbm = pl.BlockSpec(memory_space=pl.ANY)
    gcm_out, new = pl.pallas_call(
        step_kernel,
        in_specs=[whole] * 6 + [hbm],
        out_specs=[whole, hbm],
        out_shape=(sds((COLS, WIDTH), F32), sds((14848, 128), BF)),
        scratch_shapes=[
            vmem((NX, GROUP * ROWS, 128), BF),
            vmem((NX, GROUP, 2, 128, 256), BF),
            vmem((GROUP, ROWS + 8, 128), F32),
            vmem((2, 256, 256), BF),
            vmem((256, 256), BF),
            vmem((COLS, 1, 384), F32),
            vmem((COLS, 1, 384), F32),
            vmem((COLS, 1, 256), F32),
            vmem((COLS, 1, 256), F32),
            vmem((NX, NY, 256), F32),
            vmem((NX, NY, 256), F32),
            vmem((NX, NY, 256), F32),
            vmem((2, NY, 256), F32),
            vmem((2, NX, 256), F32),
            vmem((2, NX, 256), F32),
            dma((NX,)), dma((NX,)), dma, dma((NX,)), dma, dma, dma((4,)), dma((4,)),
        ],
        compiler_params=pltpu.CompilerParams(collective_id=0, has_side_effects=True, vmem_limit_bytes=VMEM_MIB * 2**20),
        name="physics_step",
    )(
        gcm_state.reshape(COLS, WIDTH), owners.reshape(1, COLS), ice_mask.reshape(COLS, CLEV),
        horizontal_operator, vertical_inverse, diffusivity.reshape(1, WIDTH), x,
    )
    new = new.reshape(7424, 2, 128).transpose(0, 2, 1).reshape(256, 3712, 2).transpose(0, 2, 1)
    return gcm_out.reshape(gcm_state.shape), new.reshape(crm_state.shape)


def solution(mesh):
    in_specs = (
        P("gx", "gy", None),
        P(("gx", "gy"), None, None, None, None),
        P(("gx", "gy"), None, None),
        P("gx", "gy", None),
        P(),
        P(),
        P(),
    )
    out_specs = (P("gx", "gy", None), P(("gx", "gy"), None, None, None, None))
    return jax.shard_map(local, mesh=mesh, in_specs=in_specs, out_specs=out_specs, check_vma=False)
```

profile of v0, /device:TPU:0, one launch (start us, length us, event | category | flops | bytes accessed | tf_op | source)
XLA Modules:
  0.0 62.1 jit_solution(8812220152077502265)
XLA Ops:
  0.6 1.4 %copy.9.v_ref = bf16[2,58,58]{2,1,0:T(8,128)(2,1)} copy(bf16[2,58,58]{2,0,1:T(2,128)(2,1)} %param.12) | data formatting | bytes 26912 | tf_op args[5]
  2.0 52.0 %physics_step.1 = (f32[128,144]{1,0:T(8,128)}, bf16[14848,128]{1,0:T(8,128)(2,1)}) custom-call(f32[128,144]{1,0:T(8,128)} %bitcast.25, s32[1,128]{1,0:T(1,128)} %bitcast.29, s32[128,58]{1,0:T(8,128)} %bitcast.27, bf16[2,64,64]{2,1,0:T(8,128)(2,1)} %h_ref.1, bf16[2,58,58]{2,1,0:T(8,128)(2,1)} %copy.9.v_ref, f32[1,144]{1,0:T(1,128)} %bitcast.28, ...), custom_call_target="tpu_custom_call" | custom-call | tf_op jit(solution)/shard_map/physics_step/pallas_call | solution.py:274
  54.0 1.6 %copy.12 = f32[8,16,144]{2,1,0:T(8,128)} copy(f32[8,16,144]{2,1,0:T(8,128)} %bitcast.26) | data formatting | bytes 147456
  55.6 6.6 %copy.13 = bf16[1,128,2,2,3712]{4,3,2,1,0:T(2,128)(2,1)} copy(bf16[1,128,2,2,3712]{4,3,2,1,0:T(2,128)(2,1)} %bitcast.24) | data formatting | bytes 7602176
where the time goes:
time: 62.5 us; the launch traced here: 62.1 us
  Pallas kernels  52 us (83%)
  local copies, waits for them, and re-layouts  9.5 us (15%)
  between operations  0.64 us (1%)
    pallas_call x1, Pallas kernels, local(): pl.pallas_call(step_kernel, in_specs=[whole] * 6 + [hbm], out_specs=[whol...  52 us
    unnamed x3, local copies, waits for them, and re-layouts  9.5 us

commit v1 on v0

--- a/solution.py
+++ b/solution.py
@@ -63,8 +63,8 @@
     for v in range(2):
         h = (h_ref[v].astype(F32) - 1.0 / 256.0).astype(BF)
         hb_ref[v] = jnp.where(diag, dot(dot(tile, h).astype(BF), tile, 1, 1), 0.0).astype(BF)
-    v0 = dot(dot(rows, v_ref[0]).astype(BF), rows, 1, 1)
-    v1 = dot(dot(rows, v_ref[1]).astype(BF), rows, 1, 1)
+    v0 = dot(dot(rows, v_ref[:, 0, :]).astype(BF), rows, 1, 1)
+    v1 = dot(dot(rows, v_ref[:, 1, :]).astype(BF), rows, 1, 1)
     vb_ref[...] = jnp.where(diag, jnp.where(a < 2, v0, v1), 0.0).astype(BF)
 
 
@@ -154,9 +154,9 @@
 
 
 def step_kernel(
-    gcm_ref, own_ref, ice_ref, h_ref, v_ref, diff_ref, x_hbm, out_ref, crm_hbm,
-    x_s, old_s, sx, hb_s, vb_s, send_s, arr_s, tend_s, ret_s, u_s, l_s, r_s, hx_s, hy_s, edge_s,
-    load_m, store_m, send_m, arr_m, back_m, ret_m, hs_m, hr_m,
+    gcm_ref, own_ref, ice_ref, h_ref, v_ref, diff_ref, x_hbm, out_ref, x_s,
+    old_s, sx, hb_s, vb_s, send_s, arr_s, tend_s, ret_s, u_s, l_s, r_s, hx_s, hy_s, edge_s,
+    load_m, send_m, arr_m, back_m, ret_m, hs_m, hr_m,
 ):
     a, b = place()
     me = a * NY + b
@@ -208,9 +208,6 @@
             settle(arr_s.at[pl.ds(0, NY - 1)], arr_m.at[slab])
 
         evolve(slab, arr_s, old_s, hb_s, vb_s, x_s, tend_s, sx)
-        pltpu.make_async_copy(
-            x_s.at[slab], crm_hbm.at[pl.ds(pl.multiple_of(slab * GROUP * ROWS, 16), GROUP * ROWS)], store_m.at[slab]
-        ).start()
         for k in range(NY):
             col = (b + k) % NY
             copy = push(tend_s.at[slab * NY + col], ret_s.at[me], back_m, ret_m, (slab, col))
@@ -254,8 +251,6 @@
     l_s[...] = pltpu.roll(u, 1, 0).reshape(NX, NY, 256)
     r_s[...] = pltpu.roll(u, COLS - 1, 0).reshape(NX, NY, 256)
     settle(tend_s.at[pl.ds(0, COLS - 1)], back_m)
-    for g in range(NX):
-        settle(x_s.at[g], store_m.at[g])
     for c in copies:
         c.wait()
     l_s[:, 0, :] = hy_s[0]
@@ -267,17 +262,16 @@
 
 
 def local(gcm_state, crm_state, owners, ice_mask, horizontal_operator, vertical_inverse, diffusivity):
-    sds, vmem, dma = jax.ShapeDtypeStruct, pltpu.VMEM, pltpu.SemaphoreType.DMA
+    vmem, dma = pltpu.VMEM, pltpu.SemaphoreType.DMA
     x = crm_state.reshape(256, 2, 3712).transpose(0, 2, 1).reshape(7424, 128, 2).transpose(0, 2, 1).reshape(14848, 128)
     whole = pl.BlockSpec(memory_space=pltpu.VMEM)
     hbm = pl.BlockSpec(memory_space=pl.ANY)
     gcm_out, new = pl.pallas_call(
         step_kernel,
         in_specs=[whole] * 6 + [hbm],
-        out_specs=[whole, hbm],
-        out_shape=(sds((COLS, WIDTH), F32), sds((14848, 128), BF)),
+        out_specs=[whole, whole],
+        out_shape=(vmem((COLS, WIDTH), F32), vmem((NX, GROUP * ROWS, 128), BF)),
         scratch_shapes=[
-            vmem((NX, GROUP * ROWS, 128), BF),
             vmem((NX, GROUP, 2, 128, 256), BF),
             vmem((GROUP, ROWS + 8, 128), F32),
             vmem((2, 256, 256), BF),
@@ -292,13 +286,13 @@
             vmem((2, NY, 256), F32),
             vmem((2, NX, 256), F32),
             vmem((2, NX, 256), F32),
-            dma((NX,)), dma((NX,)), dma, dma((NX,)), dma, dma, dma((4,)), dma((4,)),
+            dma((NX,)), dma, dma((NX,)), dma, dma, dma((4,)), dma((4,)),
         ],
         compiler_params=pltpu.CompilerParams(collective_id=0, has_side_effects=True, vmem_limit_bytes=VMEM_MIB * 2**20),
         name="physics_step",
     )(
         gcm_state.reshape(COLS, WIDTH), owners.reshape(1, COLS), ice_mask.reshape(COLS, CLEV),
-        horizontal_operator, vertical_inverse, diffusivity.reshape(1, WIDTH), x,
+        horizontal_operator, vertical_inverse.transpose(1, 0, 2), diffusivity.reshape(1, WIDTH), x,
     )
     new = new.reshape(7424, 2, 128).transpose(0, 2, 1).reshape(256, 3712, 2).transpose(0, 2, 1)
     return gcm_out.reshape(gcm_state.shape), new.reshape(crm_state.shape)

time: 62.5 us -> 54.8 us (0.88)
  local copies, waits for them, and re-layouts: 9.5 us -> 2.54 us
    unnamed x3 -> x2, local copies, waits for them, and re-layouts: 9.5 us -> 2.54 us
where the time goes in v1:
time: 54.8 us; the launch traced here: 54.6 us
  Pallas kernels  51.4 us (94%)
  local copies, waits for them, and re-layouts  2.54 us (5%)
  between operations  0.64 us (1%)
    pallas_call x1, Pallas kernels, local(): pl.pallas_call(step_kernel, in_specs=[whole] * 6 + [hbm], out_specs=[whol...  51.4 us
    unnamed x2, local copies, waits for them, and re-layouts  2.54 us

profile of v1, /device:TPU:0, one launch (start us, length us, event | category | flops | bytes accessed | tf_op | source)
XLA Modules:
  0.0 54.6 jit_solution(8833470428215999883)
XLA Ops:
  0.6 51.4 %physics_step.1 = (f32[128,144]{1,0:T(8,128)S(1)}, bf16[8,1856,128]{2,1,0:T(8,128)(2,1)S(1)}) custom-call(f32[128,144]{1,0:T(8,128)} %bitcast.27, s32[1,128]{1,0:T(1,128)} %bitcast.31, s32[128,58]{1,0:T(8,128)} %bitcast.28, bf16[2,64,64]{2,1,0:T(8,128)(2,1)} %h_ref.1, bf16[58,2,58]{2,1,0:T(2,128)(2,1)} %bitcast.29, f32[1,144]{1,0:T(1,128)} %bitcast.30, ...), custom_call_target="tpu_custom_call" | custom-call | tf_op jit(solution)/shard_map/physics_step/pallas_call | solution.py:269
  52.0 0.7 %copy.11 = f32[8,16,144]{2,1,0:T(8,128)} copy(f32[8,16,144]{2,1,0:T(8,128)S(1)} %bitcast.25) | data formatting | bytes 147456
  52.7 1.9 %copy.12 = bf16[1,128,2,2,3712]{4,3,2,1,0:T(2,128)(2,1)} copy(bf16[1,128,2,2,3712]{4,3,2,1,0:T(2,128)(2,1)S(1)} %bitcast.24) | data formatting | bytes 7602176

commit v2 on v1

--- a/solution.py
+++ b/solution.py
@@ -7,9 +7,12 @@
 
 BF, F32 = jnp.bfloat16, jnp.float32
 SUBSTEPS, CLEV, CX, LEV, COLS = 4, 58, 64, 72, 128
-BLOCKS, GROUP, ROWS = 32, 4, 464
+BLOCKS, GROUP, ROWS, CHAINS = 32, 8, 464, 4
+SOURCES, SLABS = 4 * GROUP, BLOCKS // GROUP
 NX, NY, WIDTH = 8, 16, 144
 VMEM_MIB = 58
+HALF, TWICE = (0.5, 1.0), (2.0, 1.0)
+LOG2E = 1.4426950408889634
 MESH = pl.DeviceIdType.MESH
 
 
@@ -98,40 +101,57 @@
             x0 = jnp.concatenate(
                 [jnp.concatenate([piece[j, p, 0], piece[j, p, 1]], axis=1) for j in range(2) for p in range(2)], axis=0
             )
-            old_s[g, k, v] = x0.astype(BF)
+            old_s[g, k, v] = (x0 * HALF[v]).astype(BF)
 
 
 def evolve(g, arr_s, old_s, hb_s, vb_s, x_s, tend_s, sx):
     low = iota((32, 128), 1) < 64
     ind = jnp.where(iota((8, 256), 0) == iota((8, 256), 1) // 64, 1.0, 0.0).astype(BF)
-    spread = ind[0:4, :]
-    forces, flags = [[], []], []
-    for k in range(GROUP):
-        arr = arr_s[pl.ds(g * NY + 4 * k, 4), 0, :].astype(BF)
-        for v in range(2):
-            forces[v].append(dot(arr[:, 128 * v : 128 * v + 128], spread, 0, 0) * 0.25)
-        flags.append(dot(arr[:, 256:384], spread, 0, 0))
+    lane = iota((SOURCES, 384), 1)
+    arr = arr_s[pl.ds(g * SOURCES, SOURCES), 0, :]
+    arr = jnp.where(lane < 128, 0.125 * arr, jnp.where(lane < 256, 0.25 * arr, arr)).astype(BF)
+    pick = iota((SOURCES, 256 * GROUP), 0) == iota((SOURCES, 256 * GROUP), 1) // 64
+    wide = dot(arr, jnp.where(pick, 1.0, 0.0).astype(BF), 0, 0)
+    forces = [[wide[v * 128 : (v + 1) * 128, k * 256 : (k + 1) * 256] for k in range(GROUP)] for v in range(3)]
+    flags = forces[2]
     state = [[old_s[g, k, v] for k in range(GROUP)] for v in range(2)]
-    for step in range(SUBSTEPS):
-        f = [dot(jnp.concatenate(state[v], axis=0), hb_s[v]) for v in range(2)]
-        state = [[], []]
-        for k in range(GROUP):
-            f0 = f[0][k * 128 : (k + 1) * 128] + forces[0][k]
-            f1 = f[1][k * 128 : (k + 1) * 128] + forces[1][k]
-            e = f1 - 0.5 * f0
-            soft = jnp.maximum(e, 0.0) + jnp.log(1.0 + jnp.exp(-jnp.abs(e)))
-            q = jnp.where(flags[k] > 2.5, 0.2 * e, 0.4 * soft)
-            y = jnp.concatenate([(f0 + 0.5 * q).astype(BF), (f1 - q).astype(BF)], axis=0)
+    size = GROUP // CHAINS
+
+    def across(c):
+        ks = slice(c * size, (c + 1) * size)
+        return [dot(jnp.concatenate(state[v][ks], axis=0), hb_s[v]) for v in range(2)]
+
+    def down(c, f):
+        for n in range(size):
+            k = c * size + n
+            f0 = f[0][n * 128 : (n + 1) * 128] + forces[0][k]
+            f1 = f[1][n * 128 : (n + 1) * 128] + forces[1][k]
+            e = f1 - f0
+            soft = jnp.maximum(e, 0.0) + jnp.log(1.0 + jnp.exp2(jnp.abs(e) * -LOG2E))
+            q = jnp.where(flags[k] > 2.5, 0.05 * e, 0.1 * soft)
+            y = jnp.concatenate([(f0 + q).astype(BF), (f1 - 4.0 * q).astype(BF)], axis=0)
             z = dot(vb_s[...], y).astype(BF)
             for v in range(2):
-                state[v].append(z[v * 128 : (v + 1) * 128])
+                state[v][k] = z[v * 128 : (v + 1) * 128]
+
+    held = across(0)
+    for turn in range(SUBSTEPS * CHAINS):
+        c = turn % CHAINS
+        last = turn == SUBSTEPS * CHAINS - 1
+        if CHAINS == 1:
+            down(0, held)
+            held = None if last else across(0)
+        else:
+            following = None if last else across((c + 1) % CHAINS)
+            down(c, held)
+            held = following
     for k in range(GROUP):
         old = [old_s[g, k, v] for v in range(2)]
         diff = jnp.concatenate([(state[v][k].astype(F32) - old[v].astype(F32)).astype(BF) for v in range(2)], axis=0)
-        tend = dot(ind, diff, 1, 1) * (1.0 / 64.0)
-        tend_s[pl.ds(g * NY + 4 * k, 4), 0, :] = tend[0:4].astype(BF).astype(F32)
+        tend = dot(ind, diff, 1, 1) * jnp.where(iota((8, 256), 1) < 128, 1.0 / 32.0, 1.0 / 64.0)
+        tend_s[pl.ds(g * SOURCES + 4 * k, 4), 0, :] = tend[0:4].astype(BF).astype(F32)
         for v in range(2):
-            final = jnp.where(flags[k] > 1.0, state[v][k].astype(F32), old[v].astype(F32))
+            final = jnp.where(flags[k] > 1.0, state[v][k].astype(F32), old[v].astype(F32)) * TWICE[v]
             for j in range(2):
                 for h in range(2):
                     a, b = [
@@ -154,17 +174,23 @@
 
 
 def step_kernel(
-    gcm_ref, own_ref, ice_ref, h_ref, v_ref, diff_ref, x_hbm, out_ref, x_s,
-    old_s, sx, hb_s, vb_s, send_s, arr_s, tend_s, ret_s, u_s, l_s, r_s, hx_s, hy_s, edge_s,
-    load_m, send_m, arr_m, back_m, ret_m, hs_m, hr_m,
+    gcm_hbm, own_hbm, ice_hbm, h_hbm, v_hbm, diff_hbm, x_hbm, out_ref, x_s,
+    gcm_ref, own_ref, ice_ref, h_ref, v_ref, diff_ref, old_s, sx, hb_s, vb_s, send_s, arr_s, tend_s, ret_s, u_s, l_s, r_s, hx_s, hy_s, edge_s,
+    small_m, load_m, send_m, arr_m, back_m, ret_m, hs_m, hr_m,
 ):
     a, b = place()
     me = a * NY + b
+    small = [
+        pltpu.make_async_copy(src, dst, small_m.at[n])
+        for n, (src, dst) in enumerate(
+            zip((gcm_hbm, own_hbm, ice_hbm, h_hbm, v_hbm, diff_hbm), (gcm_ref, own_ref, ice_ref, h_ref, v_ref, diff_ref))
+        )
+    ]
     loads = [
         pltpu.make_async_copy(x_hbm.at[pl.ds(g * GROUP * ROWS, GROUP * ROWS)], x_s.at[g], load_m.at[g])
-        for g in range(NX)
+        for g in range(SLABS)
     ]
-    for c in loads:
+    for c in small + loads:
         c.start()
     barrier = pltpu.get_barrier_semaphore()
 
@@ -173,6 +199,8 @@
         return carry
 
     lax.fori_loop(1, COLS, greet, 0, unroll=True)
+    for c in small:
+        c.wait()
     m0, m1 = onehots(own_ref[...], lambda o: o)
     send_s[:, 0, :] = outgoing(gcm_ref[...], ice_ref[...], m0, m1).astype(F32)
     sx[:, pl.ds(ROWS, 8), :] = jnp.zeros((GROUP, 8, 128), F32)
@@ -180,44 +208,47 @@
     operators(h_ref, v_ref, hb_s, vb_s)
     pl.semaphore_wait(barrier, COLS - 1)
 
-    def spread(g, carry):
-        row = (a + 2 * NX - 1 - g) % NX
-        for k in range(NY):
-            col = (b + k) % NY
-            copy = push(send_s.at[row * NY + col], arr_s.at[me], send_m, arr_m.at[a], (row, col))
-            if k:
-                copy.start()
-            else:
-                pl.when(g < NX - 1)(copy.start)
-        slab = (a + 1 + g) % NX
+    def send_drive(g, carry):
+        for n in range(2):
+            row = (a // 2 + 2 * SLABS - 1 - g) % SLABS * 2 + (a + n) % 2
+            for k in range(NY):
+                col = (b + k) % NY
+                copy = push(send_s.at[row * NY + col], arr_s.at[me], send_m, arr_m.at[a // 2], (row, col))
+                if n or k:
+                    copy.start()
+                else:
+                    pl.when(g < SLABS - 1)(copy.start)
+        slab = (a // 2 + 1 + g) % SLABS
         settle(x_s.at[slab], load_m.at[slab])
         unpack(slab, x_s, old_s, sx)
         return carry
 
-    lax.fori_loop(0, NX, spread, 0)
+    lax.fori_loop(0, SLABS, send_drive, 0)
 
     def group(g, carry):
-        slab = (a + 1 + g) % NX
-
-        @pl.when(g < NX - 1)
+        slab = (a // 2 + 1 + g) % SLABS
+
+        @pl.when(g < SLABS - 1)
         def _():
-            settle(arr_s.at[pl.ds(0, NY)], arr_m.at[slab])
-
-        @pl.when(g == NX - 1)
+            settle(arr_s.at[pl.ds(0, SOURCES)], arr_m.at[slab])
+
+        @pl.when(g == SLABS - 1)
         def _():
-            settle(arr_s.at[pl.ds(0, NY - 1)], arr_m.at[slab])
+            settle(arr_s.at[pl.ds(0, SOURCES - 1)], arr_m.at[slab])
 
         evolve(slab, arr_s, old_s, hb_s, vb_s, x_s, tend_s, sx)
-        for k in range(NY):
-            col = (b + k) % NY
-            copy = push(tend_s.at[slab * NY + col], ret_s.at[me], back_m, ret_m, (slab, col))
-            if k:
-                copy.start()
-            else:
-                pl.when(g < NX - 1)(copy.start)
+        for n in range(2):
+            row = slab * 2 + (a + n) % 2
+            for k in range(NY):
+                col = (b + k) % NY
+                copy = push(tend_s.at[row * NY + col], ret_s.at[me], back_m, ret_m, (row, col))
+                if n or k:
+                    copy.start()
+                else:
+                    pl.when(g < SLABS - 1)(copy.start)
         return carry
 
-    lax.fori_loop(0, NX, group, 0)
+    lax.fori_loop(0, SLABS, group, 0)
     ret_s[pl.ds(me, 1)] = tend_s[pl.ds(me, 1)]
     settle(send_s.at[pl.ds(0, COLS - 1)], send_m)
     row, col = iota((256, 256), 0), iota((256, 256), 1)
@@ -265,14 +296,16 @@
     vmem, dma = pltpu.VMEM, pltpu.SemaphoreType.DMA
     x = crm_state.reshape(256, 2, 3712).transpose(0, 2, 1).reshape(7424, 128, 2).transpose(0, 2, 1).reshape(14848, 128)
     whole = pl.BlockSpec(memory_space=pltpu.VMEM)
-    hbm = pl.BlockSpec(memory_space=pl.ANY)
+    hbm = pl.BlockSpec(memory_space=pltpu.HBM)
     gcm_out, new = pl.pallas_call(
         step_kernel,
-        in_specs=[whole] * 6 + [hbm],
+        in_specs=[hbm] * 7,
         out_specs=[whole, whole],
-        out_shape=(vmem((COLS, WIDTH), F32), vmem((NX, GROUP * ROWS, 128), BF)),
+        out_shape=(vmem((COLS, WIDTH), F32), vmem((SLABS, GROUP * ROWS, 128), BF)),
         scratch_shapes=[
-            vmem((NX, GROUP, 2, 128, 256), BF),
+            vmem((COLS, WIDTH), F32), vmem((1, COLS), jnp.int32), vmem((COLS, CLEV), jnp.int32),
+            vmem((2, CX, CX), BF), vmem((CLEV, 2, CLEV), BF), vmem((1, WIDTH), F32),
+            vmem((SLABS, GROUP, 2, 128, 256), BF),
             vmem((GROUP, ROWS + 8, 128), F32),
             vmem((2, 256, 256), BF),
             vmem((256, 256), BF),
@@ -286,7 +319,7 @@
             vmem((2, NY, 256), F32),
             vmem((2, NX, 256), F32),
             vmem((2, NX, 256), F32),
-            dma((NX,)), dma, dma((NX,)), dma, dma, dma((4,)), dma((4,)),
+            dma((6,)), dma((SLABS,)), dma, dma((SLABS,)), dma, dma, dma((4,)), dma((4,)),
         ],
         compiler_params=pltpu.CompilerParams(collective_id=0, has_side_effects=True, vmem_limit_bytes=VMEM_MIB * 2**20),
         name="physics_step",

time: 54.8 us -> 48.7 us (0.89)
  Pallas kernels: 51.4 us -> 45.4 us
    pallas_call x1, Pallas kernels: 51.4 us -> 45.4 us  [local(): pl.pallas_call(step_kernel, in_specs=[hbm] * 7, out_specs=[whole, whole],...]
where the time goes in v2:
time: 48.7 us; the launch traced here: 48.5 us
  Pallas kernels  45.4 us (93%)
  local copies, waits for them, and re-layouts  2.54 us (5%)
  between operations  0.64 us (1%)
    pallas_call x1, Pallas kernels, local(): pl.pallas_call(step_kernel, in_specs=[hbm] * 7, out_specs=[whole, whole],...  45.4 us
    unnamed x2, local copies, waits for them, and re-layouts  2.54 us

profile of v2, /device:TPU:0, one launch (start us, length us, event | category | flops | bytes accessed | tf_op | source)
XLA Modules:
  0.0 48.5 jit_solution(4666427011638896526)
XLA Ops:
  0.6 45.4 %physics_step.1 = (f32[128,144]{1,0:T(8,128)S(1)}, bf16[4,3712,128]{2,1,0:T(8,128)(2,1)S(1)}) custom-call(f32[128,144]{1,0:T(8,128)} %bitcast.27, s32[1,128]{1,0:T(1,128)} %bitcast.31, s32[128,58]{1,0:T(8,128)} %bitcast.28, bf16[2,64,64]{2,1,0:T(8,128)(2,1)} %h_hbm.1, bf16[58,2,58]{2,1,0:T(2,128)(2,1)} %bitcast.29, f32[1,144]{1,0:T(1,128)} %bitcast.30, ...), custom_call_target="tpu_custom_call" | custom-call | tf_op jit(solution)/shard_map/physics_step/pallas_call | solution.py:300
  46.0 0.7 %copy.11 = f32[8,16,144]{2,1,0:T(8,128)} copy(f32[8,16,144]{2,1,0:T(8,128)S(1)} %bitcast.25) | data formatting | bytes 147456
  46.7 1.9 %copy.12 = bf16[1,128,2,2,3712]{4,3,2,1,0:T(2,128)(2,1)} copy(bf16[1,128,2,2,3712]{4,3,2,1,0:T(2,128)(2,1)S(1)} %bitcast.24) | data formatting | bytes 7602176

commit v3 on v2

--- a/solution.py
+++ b/solution.py
@@ -145,22 +145,29 @@
             following = None if last else across((c + 1) % CHAINS)
             down(c, held)
             held = following
+    half = jnp.where(iota((8, 256), 1) < 128, 1.0 / 32.0, 1.0 / 64.0)
     for k in range(GROUP):
         old = [old_s[g, k, v] for v in range(2)]
         diff = jnp.concatenate([(state[v][k].astype(F32) - old[v].astype(F32)).astype(BF) for v in range(2)], axis=0)
-        tend = dot(ind, diff, 1, 1) * jnp.where(iota((8, 256), 1) < 128, 1.0 / 32.0, 1.0 / 64.0)
+        tend = dot(ind, diff, 1, 1) * half
         tend_s[pl.ds(g * SOURCES + 4 * k, 4), 0, :] = tend[0:4].astype(BF).astype(F32)
-        for v in range(2):
-            final = jnp.where(flags[k] > 1.0, state[v][k].astype(F32), old[v].astype(F32)) * TWICE[v]
-            for j in range(2):
-                for h in range(2):
-                    a, b = [
-                        final[(j * 2 + p) * 32 : (j * 2 + p + 1) * 32, h * 128 : (h + 1) * 128] for p in range(2)
-                    ]
-                    d = rolled(a, b, low)
-                    for i in range(2):
-                        sx[k, slot_rows(j, h, i, v, 29), :] = d[i][0:29]
-        x_s[g, pl.ds(k * ROWS, ROWS), :] = sx[k, pl.ds(0, ROWS), :].astype(BF)
+
+    def pack():
+        for k in range(GROUP):
+            old = [old_s[g, k, v] for v in range(2)]
+            for v in range(2):
+                final = jnp.where(flags[k] > 1.0, state[v][k].astype(F32), old[v].astype(F32)) * TWICE[v]
+                for j in range(2):
+                    for h in range(2):
+                        a, b = [
+                            final[(j * 2 + p) * 32 : (j * 2 + p + 1) * 32, h * 128 : (h + 1) * 128] for p in range(2)
+                        ]
+                        d = rolled(a, b, low)
+                        for i in range(2):
+                            sx[k, slot_rows(j, h, i, v, 29), :] = d[i][0:29]
+            x_s[g, pl.ds(k * ROWS, ROWS), :] = sx[k, pl.ds(0, ROWS), :].astype(BF)
+
+    return pack
 
 
 def push(src, dst, send, recv, to):
@@ -205,7 +212,6 @@
     send_s[:, 0, :] = outgoing(gcm_ref[...], ice_ref[...], m0, m1).astype(F32)
     sx[:, pl.ds(ROWS, 8), :] = jnp.zeros((GROUP, 8, 128), F32)
     arr_s[pl.ds(me, 1)] = send_s[pl.ds(me, 1)]
-    operators(h_ref, v_ref, hb_s, vb_s)
     pl.semaphore_wait(barrier, COLS - 1)
 
     def send_drive(g, carry):
@@ -224,6 +230,7 @@
         return carry
 
     lax.fori_loop(0, SLABS, send_drive, 0)
+    operators(h_ref, v_ref, hb_s, vb_s)
 
     def group(g, carry):
         slab = (a // 2 + 1 + g) % SLABS
@@ -236,16 +243,18 @@
         def _():
             settle(arr_s.at[pl.ds(0, SOURCES - 1)], arr_m.at[slab])
 
-        evolve(slab, arr_s, old_s, hb_s, vb_s, x_s, tend_s, sx)
+        pack = evolve(slab, arr_s, old_s, hb_s, vb_s, x_s, tend_s, sx)
+
+        def back(n, k):
+            row, col = slab * 2 + (a + n) % 2, (b + k) % NY
+            return push(tend_s.at[row * NY + col], ret_s.at[me], back_m, ret_m, (row, col))
+
         for n in range(2):
-            row = slab * 2 + (a + n) % 2
             for k in range(NY):
-                col = (b + k) % NY
-                copy = push(tend_s.at[row * NY + col], ret_s.at[me], back_m, ret_m, (row, col))
                 if n or k:
-                    copy.start()
-                else:
-                    pl.when(g < SLABS - 1)(copy.start)
+                    back(n, k).start()
+        pack()
+        pl.when(g < SLABS - 1)(lambda: back(0, 0).start())
         return carry
 
     lax.fori_loop(0, SLABS, group, 0)

time: 48.7 us -> 48.6 us (level)
  no operation moved by 1% of the time
where the time goes in v3:
time: 48.6 us; the launch traced here: 48.4 us
  Pallas kernels  45.2 us (93%)
  local copies, waits for them, and re-layouts  2.54 us (5%)
  between operations  0.64 us (1%)
    pallas_call x1, Pallas kernels, local(): pl.pallas_call(step_kernel, in_specs=[hbm] * 7, out_specs=[whole, whole],...  45.2 us
    unnamed x2, local copies, waits for them, and re-layouts  2.54 us

profile of v3, /device:TPU:0, one launch (start us, length us, event | category | flops | bytes accessed | tf_op | source)
XLA Modules:
  0.0 48.4 jit_solution(7288957100399461401)
XLA Ops:
  0.6 45.2 %physics_step.1 = (f32[128,144]{1,0:T(8,128)S(1)}, bf16[4,3712,128]{2,1,0:T(8,128)(2,1)S(1)}) custom-call(f32[128,144]{1,0:T(8,128)} %bitcast.27, s32[1,128]{1,0:T(1,128)} %bitcast.31, s32[128,58]{1,0:T(8,128)} %bitcast.28, bf16[2,64,64]{2,1,0:T(8,128)(2,1)} %h_hbm.1, bf16[58,2,58]{2,1,0:T(2,128)(2,1)} %bitcast.29, f32[1,144]{1,0:T(1,128)} %bitcast.30, ...), custom_call_target="tpu_custom_call" | custom-call | tf_op jit(solution)/shard_map/physics_step/pallas_call | solution.py:309
  45.9 0.7 %copy.11 = f32[8,16,144]{2,1,0:T(8,128)} copy(f32[8,16,144]{2,1,0:T(8,128)S(1)} %bitcast.25) | data formatting | bytes 147456
  46.5 1.9 %copy.12 = bf16[1,128,2,2,3712]{4,3,2,1,0:T(2,128)(2,1)} copy(bf16[1,128,2,2,3712]{4,3,2,1,0:T(2,128)(2,1)S(1)} %bitcast.24) | data formatting | bytes 7602176

commit v4 on v3

--- a/solution.py
+++ b/solution.py
@@ -183,7 +183,7 @@
 def step_kernel(
     gcm_hbm, own_hbm, ice_hbm, h_hbm, v_hbm, diff_hbm, x_hbm, out_ref, x_s,
     gcm_ref, own_ref, ice_ref, h_ref, v_ref, diff_ref, old_s, sx, hb_s, vb_s, send_s, arr_s, tend_s, ret_s, u_s, l_s, r_s, hx_s, hy_s, edge_s,
-    small_m, load_m, send_m, arr_m, back_m, ret_m, hs_m, hr_m,
+    row_m, small_m, load_m, send_m, arr_m, back_m, ret_m, hs_m, hr_m,
 ):
     a, b = place()
     me = a * NY + b
@@ -201,18 +201,20 @@
         c.start()
     barrier = pltpu.get_barrier_semaphore()
 
-    def greet(k, carry):
-        pl.semaphore_signal(barrier, inc=1, device_id=device((me + k) % COLS), device_id_type=MESH)
-        return carry
-
-    lax.fori_loop(1, COLS, greet, 0, unroll=True)
+    along_x = [(lax.rem(a + k, NX), b) for k in range(1, NX)]
+    along_y = [(a, lax.rem(b + k, NY)) for k in range(1, NY)]
+    for to in along_x + along_y:
+        pl.semaphore_signal(barrier, inc=1, device_id=to, device_id_type=MESH)
     for c in small:
         c.wait()
     m0, m1 = onehots(own_ref[...], lambda o: o)
     send_s[:, 0, :] = outgoing(gcm_ref[...], ice_ref[...], m0, m1).astype(F32)
     sx[:, pl.ds(ROWS, 8), :] = jnp.zeros((GROUP, 8, 128), F32)
     arr_s[pl.ds(me, 1)] = send_s[pl.ds(me, 1)]
-    pl.semaphore_wait(barrier, COLS - 1)
+    pl.semaphore_wait(barrier, NX + NY - 2)
+    for to in along_x:
+        pl.semaphore_signal(row_m, inc=1, device_id=to, device_id_type=MESH)
+    pl.semaphore_wait(row_m, NX - 1)
 
     def send_drive(g, carry):
         for n in range(2):
@@ -328,7 +330,7 @@
             vmem((2, NY, 256), F32),
             vmem((2, NX, 256), F32),
             vmem((2, NX, 256), F32),
-            dma((6,)), dma((SLABS,)), dma, dma((SLABS,)), dma, dma, dma((4,)), dma((4,)),
+            pltpu.SemaphoreType.REGULAR, dma((6,)), dma((SLABS,)), dma, dma((SLABS,)), dma, dma, dma((4,)), dma((4,)),
         ],
         compiler_params=pltpu.CompilerParams(collective_id=0, has_side_effects=True, vmem_limit_bytes=VMEM_MIB * 2**20),
         name="physics_step",

time: 48.6 us -> 48.3 us (level)
  no operation moved by 1% of the time
where the time goes in v4:
time: 48.3 us; the launch traced here: 48.2 us
  Pallas kernels  45 us (93%)
  local copies, waits for them, and re-layouts  2.54 us (5%)
  between operations  0.64 us (1%)
    pallas_call x1, Pallas kernels, local(): pl.pallas_call(step_kernel, in_specs=[hbm] * 7, out_specs=[whole, whole],...  45 us
    unnamed x2, local copies, waits for them, and re-layouts  2.54 us

profile of v4, /device:TPU:0, one launch (start us, length us, event | category | flops | bytes accessed | tf_op | source)
XLA Modules:
  0.0 48.2 jit_solution(868103200305747478)
XLA Ops:
  0.6 45.0 %physics_step.1 = (f32[128,144]{1,0:T(8,128)S(1)}, bf16[4,3712,128]{2,1,0:T(8,128)(2,1)S(1)}) custom-call(f32[128,144]{1,0:T(8,128)} %bitcast.27, s32[1,128]{1,0:T(1,128)} %bitcast.31, s32[128,58]{1,0:T(8,128)} %bitcast.28, bf16[2,64,64]{2,1,0:T(8,128)(2,1)} %h_hbm.1, bf16[58,2,58]{2,1,0:T(2,128)(2,1)} %bitcast.29, f32[1,144]{1,0:T(1,128)} %bitcast.30, ...), custom_call_target="tpu_custom_call" | custom-call | tf_op jit(solution)/shard_map/physics_step/pallas_call | solution.py:311
  45.6 0.7 %copy.11 = f32[8,16,144]{2,1,0:T(8,128)} copy(f32[8,16,144]{2,1,0:T(8,128)S(1)} %bitcast.25) | data formatting | bytes 147456
  46.3 1.9 %copy.12 = bf16[1,128,2,2,3712]{4,3,2,1,0:T(2,128)(2,1)} copy(bf16[1,128,2,2,3712]{4,3,2,1,0:T(2,128)(2,1)S(1)} %bitcast.24) | data formatting | bytes 7602176

commit v5 on v4

--- a/solution.py
+++ b/solution.py
@@ -205,15 +205,15 @@
     along_y = [(a, lax.rem(b + k, NY)) for k in range(1, NY)]
     for to in along_x + along_y:
         pl.semaphore_signal(barrier, inc=1, device_id=to, device_id_type=MESH)
+    pl.semaphore_wait(barrier, NX + NY - 2)
+    for to in along_x:
+        pl.semaphore_signal(row_m, inc=1, device_id=to, device_id_type=MESH)
     for c in small:
         c.wait()
     m0, m1 = onehots(own_ref[...], lambda o: o)
     send_s[:, 0, :] = outgoing(gcm_ref[...], ice_ref[...], m0, m1).astype(F32)
     sx[:, pl.ds(ROWS, 8), :] = jnp.zeros((GROUP, 8, 128), F32)
     arr_s[pl.ds(me, 1)] = send_s[pl.ds(me, 1)]
-    pl.semaphore_wait(barrier, NX + NY - 2)
-    for to in along_x:
-        pl.semaphore_signal(row_m, inc=1, device_id=to, device_id_type=MESH)
     pl.semaphore_wait(row_m, NX - 1)
 
     def send_drive(g, carry):

time: 48.3 us -> 48.3 us (level)
  no operation moved by 1% of the time
where the time goes in v5:
time: 48.3 us; the launch traced here: 48.2 us
  Pallas kernels  45 us (93%)
  local copies, waits for them, and re-layouts  2.54 us (5%)
  between operations  0.64 us (1%)
    pallas_call x1, Pallas kernels, local(): pl.pallas_call(step_kernel, in_specs=[hbm] * 7, out_specs=[whole, whole],...  45 us
    unnamed x2, local copies, waits for them, and re-layouts  2.54 us

profile of v5, /device:TPU:0, one launch (start us, length us, event | category | flops | bytes accessed | tf_op | source)
XLA Modules:
  0.0 48.2 jit_solution(10869619596193209013)
XLA Ops:
  0.6 45.0 %physics_step.1 = (f32[128,144]{1,0:T(8,128)S(1)}, bf16[4,3712,128]{2,1,0:T(8,128)(2,1)S(1)}) custom-call(f32[128,144]{1,0:T(8,128)} %bitcast.27, s32[1,128]{1,0:T(1,128)} %bitcast.31, s32[128,58]{1,0:T(8,128)} %bitcast.28, bf16[2,64,64]{2,1,0:T(8,128)(2,1)} %h_hbm.1, bf16[58,2,58]{2,1,0:T(2,128)(2,1)} %bitcast.29, f32[1,144]{1,0:T(1,128)} %bitcast.30, ...), custom_call_target="tpu_custom_call" | custom-call | tf_op jit(solution)/shard_map/physics_step/pallas_call | solution.py:311
  45.6 0.7 %copy.11 = f32[8,16,144]{2,1,0:T(8,128)} copy(f32[8,16,144]{2,1,0:T(8,128)S(1)} %bitcast.25) | data formatting | bytes 147456
  46.3 1.9 %copy.12 = bf16[1,128,2,2,3712]{4,3,2,1,0:T(2,128)(2,1)} copy(bf16[1,128,2,2,3712]{4,3,2,1,0:T(2,128)(2,1)S(1)} %bitcast.24) | data formatting | bytes 7602176
